TPU v7x, 512 devices: a whole 4x4x16 slice. The times are simulated.
512 devices in a mesh: gossip: 16 (over x, y_lo, core), zero: 32 (over z, y_hi).
Axes of the slice: x: 4, y: 4 (y_hi: 2, y_lo: 2; y = y_hi * 2 + y_lo), z: 16, core: 2. Of those that a mesh axis runs over, the one named last changes fastest.
Arguments:
- queries: bfloat16 [512, 256, 2560], P(('gossip', 'zero')), may hold values from -6 to 6
- keys: bfloat16 [512, 256, 2560], P(('gossip', 'zero')), may hold values from -6 to 6
- values: bfloat16 [512, 256, 2560], P(('gossip', 'zero')), may hold values from -24 to 24
- pattern: int32 [512, 2, 3], P(('gossip', 'zero')), may hold values from 0 to 1, as said below
- out_weight: bfloat16 [2560, 2560], P(None, 'zero'), may hold values from -0.125 to 0.125
- adapt_a: float32 [16, 2560, 64], P('gossip', 'zero'), may hold values from -5 to 5
- adapt_b: float32 [16, 64, 2560], P('gossip', None, 'zero'), may hold values from -5 to 5
Outputs:
- new_a: float32 [16, 2560, 64], P('gossip', 'zero')
- new_b: float32 [16, 64, 2560], P('gossip', None, 'zero')
Inputs may be any that keep to these rules, and one draw needn't show every extreme that they name: pattern[s, a, 0] is a; every entry of row a is at most a.
All inputs are finite; a program needn't handle non-finite values.
Results may differ from a plain program's by a relative error of at most 0.004.
Values may be sent and summed in bfloat16 or wider, within the bound.
A program may use at most 64 MiB of HBM per device.

v0:
```python
import math

import jax
import jax.numpy as jnp
from jax import lax
from jax.sharding import PartitionSpec as P

HEADS = 20
HEAD_SIZE = 128
HD = 2560
RANK = 64
DIST = 2


step_rate = 0.5
sharpness = 4.0


def shifted(block, axis, distance):
    devices = range(lax.axis_size(axis))
    route = [((i - distance) % len(devices), i) for i in devices]
    return lax.ppermute(block, axis, route)


def tile_mask(pattern, tile_size):
    count = pattern.shape[1]
    same = pattern[:, :, None] == pattern[:, None, :]
    earlier = jnp.arange(count)[None, :] < jnp.arange(count)[:, None]
    repeated = jnp.any(same & earlier[None], axis=2)
    tile_rows = jnp.arange(pattern.shape[0], dtype=jnp.int32)[:, None]
    before = (pattern < tile_rows) & ~repeated
    diagonal = (pattern == tile_rows) & ~repeated
    positions = jnp.arange(tile_size)
    causal = positions[None, :] <= positions[:, None]
    allowed = before[:, None, :, None] | diagonal[:, None, :, None] & causal[None, :, None, :]
    return allowed


def attend(queries, keys, values, pattern):
    tile_count = pattern.shape[0]
    per_row = pattern.shape[1]
    tile_size = queries.shape[0] // tile_count
    query_tiles = queries.reshape(tile_count, tile_size, HEADS, HEAD_SIZE)
    key_tiles = keys.reshape(tile_count, tile_size, HEADS, HEAD_SIZE)
    value_tiles = values.reshape(tile_count, tile_size, HEADS, HEAD_SIZE)
    flat_index = pattern.reshape(-1)
    key_chosen = jnp.take(key_tiles, flat_index, axis=0).reshape(
        tile_count, per_row, tile_size, HEADS, HEAD_SIZE
    )
    value_chosen = jnp.take(value_tiles, flat_index, axis=0).reshape(
        tile_count, per_row, tile_size, HEADS, HEAD_SIZE
    )
    scores = jnp.einsum(
        "aqhd,ajkhd->ahqjk", query_tiles, key_chosen, preferred_element_type=jnp.float32
    ) / math.sqrt(HEAD_SIZE)
    allowed = tile_mask(pattern, tile_size)[:, None]
    scores = jnp.where(allowed, scores, jnp.float32(-1e30))
    highest = jnp.max(scores, axis=(3, 4), keepdims=True)
    weights = jnp.where(allowed, jnp.exp(scores - highest), jnp.float32(0.0))
    totals = jnp.sum(weights, axis=(3, 4), keepdims=True)
    probs = (weights / totals).astype(jnp.bfloat16)
    context = jnp.einsum(
        "ahqjk,ajkhd->aqhd", probs, value_chosen, preferred_element_type=jnp.float32
    )
    return context.astype(jnp.bfloat16).reshape(tile_count * tile_size, HEADS * HEAD_SIZE)


def per_device(queries, keys, values, pattern, out_weight, adapt_a, adapt_b):
    scale_adapt = 1.0 / math.sqrt(HD * RANK)
    full_a, full_b = (
        lax.all_gather(adapt_a.astype(jnp.bfloat16), "zero", axis=1, tiled=True),
        lax.all_gather(adapt_b.astype(jnp.bfloat16), "zero", axis=2, tiled=True),
    )
    half_a = full_a[0]
    half_b = full_b[0]
    context = attend(queries[0], keys[0], values[0], pattern[0])
    adapter_low = jnp.dot(context, half_a, preferred_element_type=jnp.float32).astype(jnp.bfloat16)
    base_out = jnp.dot(
        context,
        lax.all_gather(out_weight, "zero", axis=1, tiled=True),
        preferred_element_type=jnp.float32,
    )
    output = base_out + scale_adapt * jnp.dot(
        adapter_low, half_b, preferred_element_type=jnp.float32
    )
    grad_out = jnp.tanh(sharpness * output).astype(jnp.bfloat16)
    hidden_grad = lax.dot_general(
        grad_out, half_b, (((1,), (1,)), ((), ())), preferred_element_type=jnp.float32
    ).astype(jnp.bfloat16)
    grad_a = scale_adapt * lax.dot_general(
        context, hidden_grad, (((0,), (0,)), ((), ())), preferred_element_type=jnp.float32
    )
    grad_b = scale_adapt * lax.dot_general(
        adapter_low, grad_out, (((0,), (0,)), ((), ())), preferred_element_type=jnp.float32
    )
    shard_ga, shard_gb = (
        lax.psum_scatter(grad_a, "zero", scatter_dimension=0, tiled=True),
        lax.psum_scatter(grad_b, "zero", scatter_dimension=1, tiled=True),
    )
    moved_a = adapt_a[0] - step_rate * shard_ga
    moved_b = adapt_b[0] - step_rate * shard_gb
    partner_a, partner_b = shifted((moved_a, moved_b), "gossip", DIST)
    result_a = 0.5 * (moved_a + partner_a)
    result_b = 0.5 * (moved_b + partner_b)
    return (result_a[None], result_b[None])


def solution(mesh):
    placed = (
        P(("gossip", "zero"), None, None),
        P(("gossip", "zero"), None, None),
        P(("gossip", "zero"), None, None),
        P(("gossip", "zero"), None, None),
        P(None, "zero"),
        P("gossip", "zero", None),
        P("gossip", None, "zero"),
    )
    return jax.shard_map(
        per_device,
        mesh=mesh,
        in_specs=placed,
        out_specs=(P("gossip", "zero", None), P("gossip", None, "zero")),
        check_vma=False,
    )
```

profile of v0, /device:TPU:1, one launch (start us, length us, event | category | flops | bytes accessed | tf_op | source)
XLA Modules:
  0.0 1620.8 jit_solution(8060840658676133761)
XLA Ops:
  7.2 0.7 all-gather.2.cloned.1.call-update
  7.9 0.8 reshape_squeeze.13
  8.7 2.5 reshape.104
  11.6 3.5 reshape.105
  15.1 1.7 copy.74
  16.8 3.0 gather_fusion
  19.8 3.0 gather_fusion.1
  22.9 0.8 reshape.106
  24.1 4.1 broadcast_select_fusion.1
  28.2 1.4 fusion
  29.6 2.0 fusion.1
  31.7 3.6 fusion.13
  35.3 1.4 copy.80
  36.8 83.7 %all_gather.10 = bf16[1,2560,64]{2,0,1:T(2,128)(2,1)S(1)} all-gather(bf16[1,80,64]{2,0,1:T(2,128)(2,1)S(1)} %copy.81), channel_id=1, replica_groups=mesh['gossip'=16,'zero'=32] {'zero'}, dimensions={1}, use_global_device_ids=true | all-gather | bytes 337920 | tf_op jit(solution)/shard_map/all_gather | solution.py:71
  120.5 0.8 copy.82
  121.4 78.4 %all_gather.11 = bf16[1,64,2560]{1,0,2:T(2,128)(2,1)S(1)} all-gather(bf16[1,64,80]{1,0,2:T(2,128)(2,1)S(1)} %copy.83), channel_id=1, replica_groups=mesh['gossip'=16,'zero'=32] {'zero'}, dimensions={2}, use_global_device_ids=true | all-gather | bytes 337920 | tf_op jit(solution)/shard_map/all_gather | solution.py:72
  199.8 0.8 copy.84
  200.9 74.5 %all-gather.2.cloned.1.call-done = bf16[2560,2560]{0,1:T(8,128)(2,1)} async-done(((bf16[2560,80]{0,1:T(8,128)(2,1)}), bf16[2560,2560]{0,1:T(8,128)(2,1)}) %all-gather.2.cloned.1.call-update) | async-done | bytes 13107216 | tf_op jit(solution)/shard_map/all_gather | solution.py:80
  275.5 6.7 fusion.19
  282.8 1.2 convolution_multiply_fusion.1
  284.0 2.6 copy.100
  286.7 2.4 convolution_multiply_fusion.2
  289.1 2.6 copy.98
  291.6 647.1 %reduce-scatter.9.cloned.1.call-done = f32[80,64]{1,0:T(8,128)} async-done(((f32[2560,64]{1,0:T(8,128)}), f32[80,64]{1,0:T(8,128)}) %reduce-scatter.9.cloned.1.call-update) | async-done | bytes 20496
  938.7 0.8 copy.101
  939.6 2.1 collective-permute-start.1
  941.7 664.3 %reduce-scatter.7.cloned.1.call-done = f32[80,64]{1,0:T(8,128)} async-done(((f32[2560,64]{1,0:T(8,128)}), f32[80,64]{1,0:T(8,128)}) %reduce-scatter.7.cloned.1.call-update) | async-done | bytes 20496
  1606.0 0.8 copy.99
  1606.8 2.1 collective-permute-start
  1609.0 0.6 multiply_bitcast_fusion
  1609.6 4.0 collective-permute-done
  1613.6 0.6 multiply_bitcast_fusion.1
  (31 shorter events, 2.1 us)
Async XLA Ops:
  7.2 268.3 %all-gather.2.cloned.1.call-start = ((), (), s32[]{:S(2)}) async-start(), calls=%async_computation.2 | async-start | bytes 13516800 | tf_op jit(solution)/shard_map/all_gather | solution.py:80
  7.9 930.8 %reduce-scatter.9.cloned.1.call-start = ((), (), s32[]{:S(2)}) async-start(), calls=%async_computation.4 | async-start | bytes 1351680
  19.8 3.0 copy-start
  19.8 3.9 copy-start.3
  31.7 5.0 copy-start.2
  35.3 85.9 %copy-start.1 = (f32[1,64,80]{2,1,0:T(8,128)S(1)}, f32[1,64,80]{2,1,0:T(8,128)}, u32[]{:S(2)}) copy-start(f32[1,64,80]{2,1,0:T(8,128)} %param.15) | copy-start | bytes 61444
  286.6 1319.4 %reduce-scatter.7.cloned.1.call-start = ((), (), s32[]{:S(2)}) async-start(), calls=%async_computation.3 | async-start | bytes 1351680
  939.6 669.4 %collective-permute-start.1 = (f32[64,80]{1,0:T(8,128)S(1)}, f32[64,80]{1,0:T(8,128)S(1)}, u32[]{:S(2)}, u32[]{:S(2)}) collective-permute-start(f32[64,80]{1,0:T(8,128)S(1)} %bitcast_subtract_fusion), channel_id=1, source_target_pairs={{448,0},{480,32},{0,64},{32,96},{64,128},{96,160},{128,192},{160,2... | collective-permute-start | bytes 61448 | tf_op jit(solution)/shard_map/ppermute | solution.py:22
  1606.8 6.8 collective-permute-start
Sparse Core Ops, SparseCore 0:
  11.1 264.3 all-gather.1
  286.7 651.9 reduce-scatter.8
  943.1 662.8 reduce-scatter.6
where the time goes:
time: 1630 us; the launch traced here: 1620 us
  waiting for transfers between devices  1390 us (85%)
  blocking collectives  162 us (10%)
  local copies, waits for them, and re-layouts  25.6 us (2%)
  matrix products  16.4 us (1%)
    unnamed x5, waiting for transfers between devices  1310 us
    all_gather x1, blocking collectives, per_device(): lax.all_gather(adapt_a.astype(jnp.bfloat16), 'zero', axis=1, tiled=True)  83.7 us
    all_gather x1, blocking collectives, per_device(): lax.all_gather(adapt_b.astype(jnp.bfloat16), 'zero', axis=2, tiled=True)  78.4 us
    all_gather x1, waiting for transfers between devices, per_device(): lax.all_gather(out_weight, 'zero', axis=1, tiled=True)  74.5 us
  transfers between devices with their start and end apart: 5, of which 4 were waited for; matrix products, arithmetic and copies ran while one was open for 2% of the time, Pallas kernels for 0%

commit v1 on v0

v1 whole, which is shorter than its diff:
```python
import functools
import math

import jax
import jax.numpy as jnp
from jax import lax
from jax.experimental import pallas as pl
from jax.experimental.pallas import tpu as pltpu
from jax.sharding import PartitionSpec as P

MESH = pl.DeviceIdType.MESH
HEAD = 128
TILE = 128
DIST = 2
RING = 4
STEP_RATE = 0.5
SHARPNESS = 4.0
F32 = jnp.float32
BF16 = jnp.bfloat16


def nn(a, b):
    return lax.dot_general(a, b, (((1,), (0,)), ((), ())), preferred_element_type=F32)


def nt(a, b):
    return lax.dot_general(a, b, (((1,), (1,)), ((), ())), preferred_element_type=F32)


def tn(a, b):
    return lax.dot_general(a, b, (((0,), (0,)), ((), ())), preferred_element_type=F32)


def kernel(
    nz, n_gossip, hd, rank,
    q_hbm, k_hbm, v_hbm, pattern, w_hbm, a_ref, b_ref,
    out_a, out_b,
    q, k, v, wt, ab, abf, square, mask0, mask1, ctx, low, low_t, hid, gb, grads, summed, theirs, landed, moved, partner,
    load_sem, opp_sem, zu_send, zu_recv, zd_send, zd_recv,
    right_send, left_send, left_recv, right_recv, on_send, on_recv, sib_send, sib_recv,
    abp_sem, abu_send, abu_recv, abd_send, abd_recv,
    yx_send, yx_recv, own_send, own_recv, gos_sem,
):
    half = nz // 2
    width = hd // 4
    rows = hd // (2 * nz)
    heads = hd // HEAD
    scale = 1.0 / math.sqrt(hd * rank)

    gossip, zero = lax.axis_index("gossip"), lax.axis_index("zero")
    core = lax.rem(gossip, 2)
    y_lo = lax.rem(lax.div(gossip, 2), 2)
    x = lax.div(gossip, 4)
    z = lax.div(zero, 2)
    y_hi = lax.rem(zero, 2)
    y = y_hi * 2 + y_lo
    place = core * y + (1 - core) * x

    def spread_device(step):
        xs = lax.rem(x + step + RING, RING)
        ys = lax.rem(y + step + RING, RING)
        g0, z0 = (xs * 2 + y_lo) * 2, zero
        g1, z1 = (x * 2 + lax.rem(ys, 2)) * 2 + 1, z * 2 + lax.div(ys, 2)
        return core * g1 + (1 - core) * g0, core * z1 + (1 - core) * z0

    def z_device(step):
        return gossip, lax.rem(z + step + nz, nz) * 2 + y_hi

    opposite = ((x * 2 + 1 - y_lo) * 2 + core, z * 2 + 1 - y_hi)
    sibling = ((x * 2 + y_lo) * 2 + 1 - core, zero)
    mate = (gossip, z * 2 + 1 - y_hi)
    right, left = spread_device(1), spread_device(-1)
    after = (lax.rem(gossip + DIST, n_gossip), zero)
    before = (lax.rem(gossip + n_gossip - DIST, n_gossip), zero)

    barrier = pltpu.get_barrier_semaphore()

    def greet(device):
        pl.semaphore_signal(barrier, inc=1, device_id=device, device_id_type=MESH)

    for device in (right, left, opposite, sibling, mate, after, before):
        greet(device)

    @pl.loop(1, nz)
    def _(i):
        greet(z_device(i))

    def block(step):
        p = lax.rem(place + step + RING, RING)
        return core * 2 + lax.rem(p, 2), lax.div(p, 2)

    kb, r = block(0)
    crosses = (r == y_hi) & (core == 0)

    def plane(i):
        s, odd = lax.div(i + 1, 2), lax.rem(i, 2)
        return lax.rem(z + nz + s - 2 * odd * s, nz)

    def copy(src, dst, send, recv, device):
        return pltpu.make_async_remote_copy(
            src_ref=src, dst_ref=dst, send_sem=send, recv_sem=recv, device_id=device, device_id_type=MESH
        )

    loads = [
        pltpu.make_async_copy(q_hbm.at[0], q, load_sem.at[1]),
        pltpu.make_async_copy(k_hbm.at[0], k, load_sem.at[2]),
        pltpu.make_async_copy(v_hbm.at[0], v, load_sem.at[3]),
    ]
    own = pltpu.make_async_copy(
        w_hbm.at[:, pl.ds(pl.multiple_of(kb * width, 128), width)], wt.at[kb, z, r], load_sem.at[0]
    )

    @pl.when(r == y_hi)
    def _():
        own.start()

    for load in loads:
        load.start()

    square[...] = jnp.zeros_like(square)
    square[0:rank, 0:rows] = a_ref[0]
    square[rank:, 0:rows] = b_ref[0]
    abf[...] = square[...].T[0:rows]
    ab[z, y_hi] = abf[...].astype(BF16)

    key_at = lax.broadcasted_iota(jnp.int32, (TILE, 2 * TILE), 0)
    query_at = lax.broadcasted_iota(jnp.int32, (TILE, 2 * TILE), 1)
    sees = (pattern[0, 1, 1] == 0) | (pattern[0, 1, 2] == 0)
    far = jnp.where(sees, F32(0.0), F32(-1e30))
    mask0[...] = jnp.where(query_at < TILE, jnp.where(key_at <= query_at, F32(0.0), F32(-1e30)), far)
    mask1[...] = jnp.where(key_at <= query_at, F32(0.0), F32(-1e30))[:, 0:TILE]

    @pl.when(r == y_hi)
    def _():
        own.wait()

    pl.semaphore_wait(barrier, nz - 1 + 7)

    def cross():
        return copy(wt.at[kb, z, r], wt.at[kb, z, r], opp_sem.at[0], opp_sem.at[1], opposite)

    def up(s):
        at = wt.at[kb, lax.rem(z - s + nz, nz), r]
        return copy(at, at, zu_send.at[s], zu_recv.at[s + 1], z_device(1))

    def up_in(s):
        at = wt.at[kb, lax.rem(z - s + nz, nz), r]
        return copy(at, at, zu_send.at[s], zu_recv.at[s], z_device(1))

    def down(s):
        at = wt.at[kb, lax.rem(z + s, nz), r]
        return copy(at, at, zd_send.at[s], zd_recv.at[s + 1], z_device(-1))

    def down_in(s):
        at = wt.at[kb, lax.rem(z + s, nz), r]
        return copy(at, at, zd_send.at[s], zd_recv.at[s], z_device(-1))

    def to_right(i):
        at = wt.at[kb, plane(i), r]
        return copy(at, at, right_send.at[i], left_recv.at[i], right)

    def to_left(i):
        at = wt.at[kb, plane(i), r]
        return copy(at, at, left_send.at[i], right_recv.at[i], left)

    def from_left(i):
        n, m = block(-1)
        at = wt.at[n, plane(i), m]
        return copy(at, at, on_send.at[i], left_recv.at[i], right)

    def from_right(i):
        n, m = block(1)
        at = wt.at[n, plane(i), m]
        return copy(at, at, on_send.at[i], right_recv.at[i], left)

    def on_right(i):
        n, m = block(-1)
        at = wt.at[n, plane(i), m]
        return copy(at, at, on_send.at[i], on_recv.at[i], right)

    def on_left(i):
        n, m = block(1)
        at = wt.at[n, plane(i), m]
        return copy(at, at, on_send.at[i], on_recv.at[i], left)

    def on_in(i):
        n, m = block(2)
        at = wt.at[n, plane(i), m]
        return copy(at, at, on_send.at[i], on_recv.at[i], right)

    def across(i):
        at = wt.at[pl.ds(core * 2, 2), plane(i)]
        return copy(at, at, sib_send.at[i], sib_recv.at[i], sibling)

    def across_in(i):
        at = wt.at[pl.ds(2 - core * 2, 2), plane(i)]
        return copy(at, at, sib_send.at[i], sib_recv.at[i], sibling)

    def spread(i):
        to_right(i).start()
        to_left(i).start()

    def arrive(s):
        up_in(s).wait_recv()
        if s < half:
            up(s).start()
        spread(2 * s - 1)
        if s < half:
            down_in(s).wait_recv()
            if s < half - 1:
                down(s).start()
            spread(2 * s)

    def hand_on(s):
        i = max(2 * s - 1, 0)
        from_left(i).wait_recv()
        on_right(i).start()
        from_right(i).wait_recv()
        if 0 < s < half:
            from_right(2 * s).wait_recv()
            on_left(2 * s).start()
            from_left(2 * s).wait_recv()

    def share(s):
        on_in(max(2 * s - 1, 0)).wait_recv()
        across(max(2 * s - 1, 0)).start()
        if 0 < s < half:
            on_in(2 * s).wait_recv()
            across(2 * s).start()

    def ab_mate(which):
        at = ab.at[z, which]
        return copy(at, at, abp_sem.at[0], abp_sem.at[1], mate)

    def ab_up(s, slot):
        at = ab.at[lax.rem(z - s + nz, nz)]
        return copy(at, at, abu_send.at[s], abu_recv.at[slot], z_device(1))

    def ab_down(s, slot):
        at = ab.at[lax.rem(z + s, nz)]
        return copy(at, at, abd_send.at[s], abd_recv.at[slot], z_device(-1))

    def ab_step(s):
        ab_up(s, s).wait_recv()
        if s < half:
            ab_up(s, s + 1).start()
            ab_down(s, s).wait_recv()
            if s < half - 1:
                ab_down(s, s + 1).start()

    fold = F32(math.log2(math.e) / math.sqrt(HEAD))

    def attend(first, last):
        @pl.loop(first, last)
        def _(h):
            at = pl.ds(pl.multiple_of(h * HEAD, HEAD), HEAD)
            qh = q[:, at]
            s0 = nt(k[0:TILE, at], qh) * fold + mask0[...]
            s1 = nt(k[TILE:, at], qh[TILE:]) * fold + mask1[...]
            top0 = jnp.max(s0, axis=0, keepdims=True)
            top1 = jnp.max(s1, axis=0, keepdims=True)
            top1 = jnp.maximum(top0[:, TILE:], top1)
            e00 = jnp.exp2(s0[:, 0:TILE] - top0[:, 0:TILE])
            e01 = jnp.exp2(s0[:, TILE:] - top1)
            e11 = jnp.exp2(s1 - top1)
            total0 = jnp.sum(e00, axis=0, keepdims=True)
            total1 = jnp.sum(e01, axis=0, keepdims=True) + jnp.sum(e11, axis=0, keepdims=True)
            v0, v1 = v[0:TILE, at], v[TILE:, at]
            c0 = tn(v0, e00.astype(BF16)) / total0
            c1 = (tn(v0, e01.astype(BF16)) + tn(v1, e11.astype(BF16))) / total1
            ctx[at, 0:TILE] = c0.astype(BF16)
            ctx[at, TILE:] = c1.astype(BF16)

    def project(first, last):
        @pl.loop(first, last)
        def _(i):
            across_in(i).wait_recv()
            w = plane(i)
            factors = ab[w].reshape(2 * rows, 2 * rank)
            out = scale * nn(factors, low[...])
            for n in range(4):
                out += nn(wt[n, w].reshape(2 * rows, width), ctx[n * width : (n + 1) * width])
            slope = jnp.tanh(SHARPNESS * out).astype(BF16)
            hid[...] += tn(factors, slope)
            gb[w] = nn(slope, low_t[...])

    @pl.when(crosses)
    def _():
        cross().start()

    ab_mate(y_hi).start()

    @pl.when(r != y_hi)
    def _():
        cross().wait_recv()

    up(0).start()
    down(0).start()
    spread(0)
    for load in loads:
        load.wait()
    hid[...] = jnp.zeros_like(hid)
    cut = [heads * n // 4 for n in range(5)]
    ab_mate(1 - y_hi).wait_recv()
    ab_up(0, 1).start()
    ab_down(0, 1).start()

    def ab_steps(first, last):
        for s in range(first, last):
            if s <= half:
                ab_step(s)

    attend(cut[0], cut[1])
    ab_steps(1, 2)
    arrive(1)
    hand_on(0)
    attend(cut[1], cut[2])
    ab_steps(2, 3)
    share(0)
    attend(cut[2], cut[3])
    ab_steps(3, 4)
    if half >= 2:
        arrive(2)
    hand_on(1)
    attend(cut[3], cut[4])
    ab_steps(4, 6)
    share(1)
    if half >= 3:
        arrive(3)
    if half >= 2:
        hand_on(2)
        share(2)
    ab_steps(6, 9)

    both = tn(ab[...].reshape(hd, 2 * rank), ctx[...])
    low[0:rank] = jnp.zeros((rank, 2 * TILE), BF16)
    low[rank:] = both[0:rank].astype(BF16)
    low_t[...] = low[...].astype(F32).T.astype(BF16)

    done = 0

    def project_to(s):
        nonlocal done
        last = min(2 * s + 1, nz)
        if last > done:
            project(done, last)
            done = last

    for s in range(4, half + 1):
        arrive(s)
        project_to(2 * (s - 4) + (s > 4) if s < 6 else s - 2)
        hand_on(s - 1)
        share(s - 1)
    if half >= 3:
        project_to(half - 1)
        hand_on(half)
        share(half)
    project_to(half)

    square[...] = jnp.zeros_like(square)
    hid_t = jnp.concatenate([hid[rank:], jnp.zeros((rank, 2 * TILE), F32)], axis=0).T.astype(BF16)

    def trade(i):
        w = plane(i)
        return copy(grads.at[w, 1 - y_hi], theirs.at[w], yx_send.at[i], yx_recv.at[i], mate)

    def give(i):
        w = plane(i)
        return copy(summed.at[w], landed.at[z], own_send.at[i], own_recv.at[z], (gossip, w * 2 + y_hi))

    def take(i):
        w = plane(i)
        return copy(summed.at[w], landed.at[w], own_send.at[i], own_recv.at[w], (gossip, w * 2 + y_hi))

    @pl.loop(0, nz)
    def _(n):
        i = nz - 1 - n
        w = plane(i)
        part = ctx[pl.ds(pl.multiple_of(w * 2 * rows, 2 * rows), 2 * rows)]
        both = scale * (nn(part, hid_t) + gb[w])
        grads[w] = both.astype(BF16).reshape(2, rows, 2 * rank)
        trade(i).start()

    @pl.loop(0, nz - 1)
    def _(n):
        i = nz - 1 - n
        w = plane(i)
        trade(i).wait_recv()
        summed[w] = (grads[w, y_hi].astype(F32) + theirs[w].astype(F32)).astype(BF16)
        give(i).start()

    trade(0).wait_recv()
    moved[...] = grads[z, y_hi].astype(F32) + theirs[z].astype(F32)

    @pl.loop(1, nz)
    def _(i):
        take(i).wait_recv()
        moved[...] += landed[plane(i)].astype(F32)

    moved[...] = abf[...] - STEP_RATE * moved[...]
    gossip_copy = copy(moved, partner, gos_sem.at[0], gos_sem.at[1], after)
    gossip_copy.start()
    gossip_copy.wait_recv()
    new = 0.5 * (moved[...] + partner[...])
    square[0:rows] = new
    turned = square[...].T
    out_a[0] = turned[0:rank, 0:rows]
    out_b[0] = turned[rank:, 0:rows]

    gossip_copy.wait_send()

    @pl.when(crosses)
    def _():
        cross().wait_send()

    ab_mate(y_hi).wait_send()

    @pl.loop(0, half)
    def _(s):
        up(s).wait_send()
        ab_up(s, s + 1).wait_send()

    @pl.loop(0, half - 1)
    def _(s):
        down(s).wait_send()
        ab_down(s, s + 1).wait_send()

    @pl.loop(0, nz)
    def _(i):
        to_right(i).wait_send()
        to_left(i).wait_send()
        on_in(i).wait_send()
        across(i).wait_send()
        trade(i).wait_send()

    @pl.loop(1, nz)
    def _(i):
        give(i).wait_send()


def solution(mesh):
    n_gossip, n_zero = mesh.shape["gossip"], mesh.shape["zero"]
    nz = n_zero // 2
    half = nz // 2

    def per_device(queries, keys, values, pattern, out_weight, adapt_a, adapt_b):
        _, tokens, hd = queries.shape
        rows, rank = adapt_a.shape[1:]
        width = hd // 4
        dma = pltpu.SemaphoreType.DMA
        vmem = pltpu.VMEM
        whole = pl.BlockSpec(memory_space=pltpu.VMEM)
        place = pl.BlockSpec(memory_space=pl.ANY)
        flops = 2 * tokens * hd * (hd + 2 * tokens + 4 * rank)
        new_a, new_b = pl.pallas_call(
            functools.partial(kernel, nz, n_gossip, hd, rank),
            out_shape=(
                jax.ShapeDtypeStruct((1, rank, rows), F32),
                jax.ShapeDtypeStruct((1, rank, rows), F32),
            ),
            in_specs=[place, place, place, pl.BlockSpec(memory_space=pltpu.SMEM), place, whole, whole],
            out_specs=(whole, whole),
            scratch_shapes=[
                vmem((tokens, hd), BF16), vmem((tokens, hd), BF16), vmem((tokens, hd), BF16),
                vmem((4, nz, 2, rows, width), BF16),
                vmem((nz, 2, rows, 2 * rank), BF16), vmem((rows, 2 * rank), F32), vmem((2 * rank, 128), F32),
                vmem((TILE, 2 * TILE), F32), vmem((TILE, TILE), F32),
                vmem((hd, tokens), BF16), vmem((2 * rank, tokens), BF16), vmem((tokens, 2 * rank), BF16),
                vmem((2 * rank, tokens), F32), vmem((nz, 2 * rows, 2 * rank), F32),
                vmem((nz, 2, rows, 2 * rank), BF16), vmem((nz, rows, 2 * rank), BF16),
                vmem((nz, rows, 2 * rank), BF16), vmem((nz, rows, 2 * rank), BF16),
                vmem((rows, 2 * rank), F32), vmem((rows, 2 * rank), F32),
                dma((4,)), dma((2,)),
                dma((half + 1,)), dma((half + 1,)), dma((half + 1,)), dma((half + 1,)),
                dma((nz,)), dma((nz,)), dma((nz,)), dma((nz,)), dma((nz,)), dma((nz,)), dma((nz,)), dma((nz,)),
                dma((2,)), dma((half + 1,)), dma((half + 1,)), dma((half + 1,)), dma((half + 1,)),
                dma((nz,)), dma((nz,)), dma((nz,)), dma((nz,)), dma((2,)),
            ],
            compiler_params=pltpu.CompilerParams(
                collective_id=0, has_side_effects=True, vmem_limit_bytes=60 * 1024 * 1024
            ),
            cost_estimate=pl.CostEstimate(flops=flops, bytes_accessed=8 * tokens * hd, transcendentals=tokens * hd),
        )(queries, keys, values, pattern, out_weight.T, adapt_a.transpose(0, 2, 1), adapt_b)
        return new_a.transpose(0, 2, 1), new_b

    placed = (
        P(("gossip", "zero"), None, None),
        P(("gossip", "zero"), None, None),
        P(("gossip", "zero"), None, None),
        P(("gossip", "zero"), None, None),
        P(None, "zero"),
        P("gossip", "zero", None),
        P("gossip", None, "zero"),
    )
    return jax.shard_map(
        per_device,
        mesh=mesh,
        in_specs=placed,
        out_specs=(P("gossip", "zero", None), P("gossip", None, "zero")),
        check_vma=False,
    )
```

time: 1630 us -> 129 us (0.08)
  waiting for transfers between devices: 1390 us -> 0 us
  blocking collectives: 162 us -> 0 us
  Pallas kernels: 0 us -> 125 us
  local copies, waits for them, and re-layouts: 25.6 us -> 2.75 us
  matrix products: 16.4 us -> 0 us
    unnamed x5 -> x0, waiting for transfers between devices: 1310 us -> none
    all_gather x2 -> x0, blocking collectives: 162 us -> none  [the longest x1 83.7 us: per_device(): lax.all_gather(adapt_a.astype(jnp.bfloat16), 'zero', axis=1, tiled=True)]
    pallas_call x0 -> x1, Pallas kernels: none -> 125 us  [per_device(): pl.pallas_call(functools.partial(kernel, nz, n_gossip, hd, rank), out_sha...]
    all_gather x1 -> x0, waiting for transfers between devices: 74.5 us -> none  [per_device(): lax.all_gather(out_weight, 'zero', axis=1, tiled=True)]
    dot_general x7 -> x0, matrix products: 16.4 us -> none  [the longest x1 6.71 us: per_device(): jnp.dot(context, lax.all_gather(out_weight, 'zero', axis=1, tiled=True),...]
  transfers between devices with their start and end apart: 5 -> 0, of which waited for: 4 -> 0; matrix products, arithmetic and copies ran while one was open for 2% -> 0% of each run, Pallas kernels for 0% -> 0%
where the time goes in v1:
time: 129 us
  Pallas kernels  125 us (97%)
  local copies, waits for them, and re-layouts  2.75 us (2%)
    pallas_call x1, Pallas kernels, per_device(): pl.pallas_call(functools.partial(kernel, nz, n_gossip, hd, rank), out_sha...  125 us
    unnamed x2, local copies, waits for them, and re-layouts  2.75 us

profile of v1, /device:TPU:1, one launch (start us, length us, event | category | flops | bytes accessed | tf_op | source)
XLA Modules:
  0.0 128.7 jit_solution(1214958071287188561)
XLA Ops:
  0.6 125.3 %shard_map.86 = (f32[1,64,80]{2,1,0:T(8,128)}, f32[1,64,80]{2,1,0:T(8,128)}) custom-call(bf16[1,256,2560]{2,1,0:T(8,128)(2,1)} %q_hbm.1, bf16[1,256,2560]{2,1,0:T(8,128)(2,1)} %k_hbm.1, bf16[1,256,2560]{2,1,0:T(8,128)(2,1)} %v_hbm.1, s32[1,2,3]{2,1,0:T(2,128)} %pattern.1, bf16[80,2560]{1,0:T(8,128)(2,1)} %bitcast.4, f32[1,64,80]{2,1,0:T(8,128)} %bitcast.5, ...), custom_call_target="tpu_custom_call" | custom-call | flops 4362076160 | bytes 5242880 | tf_op jit(solution)/shard_map/pallas_call | solution.py:455
  126.0 1.4 %copy.11 = f32[1,80,64]{1,2,0:T(8,128)} copy(f32[1,80,64]{1,2,0:T(8,128)} %bitcast.3) | data formatting | bytes 40960
  127.4 1.4 %copy.12 = f32[1,64,80]{2,1,0:T(8,128)} copy(f32[1,64,80]{2,1,0:T(8,128)} %get-tuple-element.9) | data formatting | bytes 40960

commit v2 on v1

--- a/solution.py
+++ b/solution.py
@@ -1,4 +1,5 @@
 import functools
+import itertools
 import math
 
 import jax
@@ -42,6 +43,8 @@
     yx_send, yx_recv, own_send, own_recv, gos_sem,
 ):
     half = nz // 2
+    jump = half // 2 if half >= 4 else 0
+    firsts = (1, jump) if jump else (1,)
     width = hd // 4
     rows = hd // (2 * nz)
     heads = hd // HEAD
@@ -78,12 +81,11 @@
     def greet(device):
         pl.semaphore_signal(barrier, inc=1, device_id=device, device_id_type=MESH)
 
-    for device in (right, left, opposite, sibling, mate, after, before):
+    partners = [right, left, opposite, sibling, mate, after, before]
+    for s in firsts:
+        partners += [z_device(s), z_device(-s)] if 2 * s != nz else [z_device(s)]
+    for device in partners:
         greet(device)
-
-    @pl.loop(1, nz)
-    def _(i):
-        greet(z_device(i))
 
     def block(step):
         p = lax.rem(place + step + RING, RING)
@@ -134,22 +136,22 @@
     def _():
         own.wait()
 
-    pl.semaphore_wait(barrier, nz - 1 + 7)
+    pl.semaphore_wait(barrier, len(partners))
 
     def cross():
         return copy(wt.at[kb, z, r], wt.at[kb, z, r], opp_sem.at[0], opp_sem.at[1], opposite)
 
-    def up(s):
+    def up(s, step=1):
         at = wt.at[kb, lax.rem(z - s + nz, nz), r]
-        return copy(at, at, zu_send.at[s], zu_recv.at[s + 1], z_device(1))
+        return copy(at, at, zu_send.at[s + step], zu_recv.at[s + step], z_device(step))
 
     def up_in(s):
         at = wt.at[kb, lax.rem(z - s + nz, nz), r]
         return copy(at, at, zu_send.at[s], zu_recv.at[s], z_device(1))
 
-    def down(s):
+    def down(s, step=1):
         at = wt.at[kb, lax.rem(z + s, nz), r]
-        return copy(at, at, zd_send.at[s], zd_recv.at[s + 1], z_device(-1))
+        return copy(at, at, zd_send.at[s + step], zd_recv.at[s + step], z_device(-step))
 
     def down_in(s):
         at = wt.at[kb, lax.rem(z + s, nz), r]
@@ -202,12 +204,12 @@
 
     def arrive(s):
         up_in(s).wait_recv()
-        if s < half:
+        if s < half and s + 1 not in firsts:
             up(s).start()
         spread(2 * s - 1)
         if s < half:
             down_in(s).wait_recv()
-            if s < half - 1:
+            if s < half - 1 and s + 1 not in firsts:
                 down(s).start()
             spread(2 * s)
 
@@ -232,21 +234,24 @@
         at = ab.at[z, which]
         return copy(at, at, abp_sem.at[0], abp_sem.at[1], mate)
 
-    def ab_up(s, slot):
+    def ab_up(s, step=1):
         at = ab.at[lax.rem(z - s + nz, nz)]
-        return copy(at, at, abu_send.at[s], abu_recv.at[slot], z_device(1))
-
-    def ab_down(s, slot):
+        return copy(at, at, abu_send.at[s + step], abu_recv.at[s + step], z_device(step))
+
+    def ab_down(s, step=1):
         at = ab.at[lax.rem(z + s, nz)]
-        return copy(at, at, abd_send.at[s], abd_recv.at[slot], z_device(-1))
-
-    def ab_step(s):
-        ab_up(s, s).wait_recv()
+        return copy(at, at, abd_send.at[s + step], abd_recv.at[s + step], z_device(-step))
+
+    def ab_in(s):
+        at = ab.at[lax.rem(z - s + nz, nz)]
+        copy(at, at, abu_send.at[s], abu_recv.at[s], z_device(1)).wait_recv()
+        if s < half and s + 1 not in firsts:
+            ab_up(s).start()
         if s < half:
-            ab_up(s, s + 1).start()
-            ab_down(s, s).wait_recv()
-            if s < half - 1:
-                ab_down(s, s + 1).start()
+            at = ab.at[lax.rem(z + s, nz)]
+            copy(at, at, abd_send.at[s], abd_recv.at[s], z_device(-1)).wait_recv()
+            if s < half - 1 and s + 1 not in firsts:
+                ab_down(s).start()
 
     fold = F32(math.log2(math.e) / math.sqrt(HEAD))
 
@@ -271,18 +276,24 @@
             ctx[at, 0:TILE] = c0.astype(BF16)
             ctx[at, TILE:] = c1.astype(BF16)
 
-    def project(first, last):
-        @pl.loop(first, last)
-        def _(i):
+    def project(s):
+        members = [max(2 * s - 1, 0)] + ([2 * s] if 0 < s < half else [])
+        for i in members:
             across_in(i).wait_recv()
-            w = plane(i)
-            factors = ab[w].reshape(2 * rows, 2 * rank)
-            out = scale * nn(factors, low[...])
-            for n in range(4):
-                out += nn(wt[n, w].reshape(2 * rows, width), ctx[n * width : (n + 1) * width])
-            slope = jnp.tanh(SHARPNESS * out).astype(BF16)
-            hid[...] += tn(factors, slope)
-            gb[w] = nn(slope, low_t[...])
+        planes = [plane(i) for i in members]
+
+        def rows_of(blocks):
+            return jnp.concatenate([b.reshape(2 * rows, b.shape[-1]) for b in blocks], axis=0)
+
+        factors = rows_of([ab[w] for w in planes])
+        out = scale * nn(factors, low[...])
+        for n in range(4):
+            out += nn(rows_of([wt[n, w] for w in planes]), ctx[n * width : (n + 1) * width])
+        slope = jnp.tanh(SHARPNESS * out).astype(BF16)
+        hid[...] += tn(factors, slope)
+        second = nn(slope, low_t[...])
+        for n, w in enumerate(planes):
+            gb[w] = second[n * 2 * rows : (n + 1) * 2 * rows]
 
     @pl.when(crosses)
     def _():
@@ -294,68 +305,59 @@
     def _():
         cross().wait_recv()
 
-    up(0).start()
-    down(0).start()
+    for s in reversed(firsts):
+        up(0, s).start()
+        if s < half:
+            down(0, s).start()
     spread(0)
     for load in loads:
         load.wait()
     hid[...] = jnp.zeros_like(hid)
-    cut = [heads * n // 4 for n in range(5)]
+    cut = [heads * n // 5 for n in range(6)]
+    attend(cut[0], cut[1])
     ab_mate(1 - y_hi).wait_recv()
-    ab_up(0, 1).start()
-    ab_down(0, 1).start()
-
-    def ab_steps(first, last):
-        for s in range(first, last):
-            if s <= half:
-                ab_step(s)
-
-    attend(cut[0], cut[1])
-    ab_steps(1, 2)
-    arrive(1)
-    hand_on(0)
+    for s in reversed(firsts):
+        ab_up(0, s).start()
+        if s < half:
+            ab_down(0, s).start()
     attend(cut[1], cut[2])
-    ab_steps(2, 3)
-    share(0)
-    attend(cut[2], cut[3])
-    ab_steps(3, 4)
-    if half >= 2:
-        arrive(2)
-    hand_on(1)
-    attend(cut[3], cut[4])
-    ab_steps(4, 6)
-    share(1)
-    if half >= 3:
-        arrive(3)
-    if half >= 2:
-        hand_on(2)
-        share(2)
-    ab_steps(6, 9)
+    chains = [range(a, b) for a, b in zip(firsts, (*firsts[1:], half + 1))]
+    ticks = [[s for s in tick if s is not None] for tick in itertools.zip_longest(*chains)]
+    stages = [[0], *ticks]
+    for n, tick in enumerate(ticks):
+        for s in tick:
+            arrive(s)
+        for s in tick:
+            ab_in(s)
+        if n < 3:
+            attend(cut[n + 2], cut[n + 3])
+        for s in stages[n]:
+            hand_on(s)
+        for s in stages[n - 1] if n else ():
+            share(s)
+    for n in range(len(ticks), 3):
+        attend(cut[n + 2], cut[n + 3])
 
     both = tn(ab[...].reshape(hd, 2 * rank), ctx[...])
     low[0:rank] = jnp.zeros((rank, 2 * TILE), BF16)
     low[rank:] = both[0:rank].astype(BF16)
     low_t[...] = low[...].astype(F32).T.astype(BF16)
 
-    done = 0
-
-    def project_to(s):
-        nonlocal done
-        last = min(2 * s + 1, nz)
-        if last > done:
-            project(done, last)
-            done = last
-
-    for s in range(4, half + 1):
-        arrive(s)
-        project_to(2 * (s - 4) + (s > 4) if s < 6 else s - 2)
-        hand_on(s - 1)
-        share(s - 1)
-    if half >= 3:
-        project_to(half - 1)
-        hand_on(half)
-        share(half)
-    project_to(half)
+    todo = [s for tick in stages[:-2] for s in tick]
+    later = stages[-2]
+    third = len(todo) // 3
+    for s in todo[:third]:
+        project(s)
+    for s in stages[-1]:
+        hand_on(s)
+    for s in later:
+        share(s)
+    for s in todo[third : 2 * third]:
+        project(s)
+    for s in stages[-1]:
+        share(s)
+    for s in [*todo[2 * third :], *later, *stages[-1]]:
+        project(s)
 
     square[...] = jnp.zeros_like(square)
     hid_t = jnp.concatenate([hid[rank:], jnp.zeros((rank, 2 * TILE), F32)], axis=0).T.astype(BF16)
@@ -418,12 +420,12 @@
     @pl.loop(0, half)
     def _(s):
         up(s).wait_send()
-        ab_up(s, s + 1).wait_send()
+        ab_up(s).wait_send()
 
     @pl.loop(0, half - 1)
     def _(s):
         down(s).wait_send()
-        ab_down(s, s + 1).wait_send()
+        ab_down(s).wait_send()
 
     @pl.loop(0, nz)
     def _(i):

time: 129 us -> 98.2 us (0.76)
  the two profiles are of different devices: /device:TPU:1 before, /device:TPU:16 now
where the time goes in v2:
time: 98.2 us; the launch traced here: 97.9 us
  Pallas kernels  94.5 us (96%)
  local copies, waits for them, and re-layouts  2.75 us (3%)
    pallas_call x1, Pallas kernels, per_device(): pl.pallas_call(functools.partial(kernel, nz, n_gossip, hd, rank), out_sha...  94.5 us
    unnamed x2, local copies, waits for them, and re-layouts  2.75 us

profile of v2, /device:TPU:16, one launch (start us, length us, event | category | flops | bytes accessed | tf_op | source)
XLA Modules:
  0.0 97.9 jit_solution(17316680541574002199)
XLA Ops:
  0.6 94.5 %shard_map.86 = (f32[1,64,80]{2,1,0:T(8,128)}, f32[1,64,80]{2,1,0:T(8,128)}) custom-call(bf16[1,256,2560]{2,1,0:T(8,128)(2,1)} %q_hbm.1, bf16[1,256,2560]{2,1,0:T(8,128)(2,1)} %k_hbm.1, bf16[1,256,2560]{2,1,0:T(8,128)(2,1)} %v_hbm.1, s32[1,2,3]{2,1,0:T(2,128)} %pattern.1, bf16[80,2560]{1,0:T(8,128)(2,1)} %bitcast.4, f32[1,64,80]{2,1,0:T(8,128)} %bitcast.5, ...), custom_call_target="tpu_custom_call" | custom-call | flops 4362076160 | bytes 5242880 | tf_op jit(solution)/shard_map/pallas_call | solution.py:457
  95.1 1.4 %copy.11 = f32[1,80,64]{1,2,0:T(8,128)} copy(f32[1,80,64]{1,2,0:T(8,128)} %bitcast.3) | data formatting | bytes 40960
  96.5 1.4 %copy.12 = f32[1,64,80]{2,1,0:T(8,128)} copy(f32[1,64,80]{2,1,0:T(8,128)} %get-tuple-element.9) | data formatting | bytes 40960

commit v3 on v2

--- a/solution.py
+++ b/solution.py
@@ -14,6 +14,7 @@
 TILE = 128
 DIST = 2
 RING = 4
+PLAN = ((3, 0), (2, 0), (1, 3), (1, 1))
 STEP_RATE = 0.5
 SHARPNESS = 4.0
 F32 = jnp.float32
@@ -35,8 +36,8 @@
 def kernel(
     nz, n_gossip, hd, rank,
     q_hbm, k_hbm, v_hbm, pattern, w_hbm, a_ref, b_ref,
-    out_a, out_b,
-    q, k, v, wt, ab, abf, square, mask0, mask1, ctx, low, low_t, hid, gb, grads, summed, theirs, landed, moved, partner,
+    out,
+    q, k, v, wt, ab, abf, square, mask0, mask1, ctx, low, low_t, base, hid, grads, summed, theirs, landed, total, moved, partner,
     load_sem, opp_sem, zu_send, zu_recv, zd_send, zd_recv,
     right_send, left_send, left_recv, right_recv, on_send, on_recv, sib_send, sib_recv,
     abp_sem, abu_send, abu_recv, abd_send, abd_recv,
@@ -141,21 +142,16 @@
     def cross():
         return copy(wt.at[kb, z, r], wt.at[kb, z, r], opp_sem.at[0], opp_sem.at[1], opposite)
 
-    def up(s, step=1):
-        at = wt.at[kb, lax.rem(z - s + nz, nz), r]
-        return copy(at, at, zu_send.at[s + step], zu_recv.at[s + step], z_device(step))
-
-    def up_in(s):
-        at = wt.at[kb, lax.rem(z - s + nz, nz), r]
-        return copy(at, at, zu_send.at[s], zu_recv.at[s], z_device(1))
-
-    def down(s, step=1):
-        at = wt.at[kb, lax.rem(z + s, nz), r]
-        return copy(at, at, zd_send.at[s + step], zd_recv.at[s + step], z_device(-step))
-
-    def down_in(s):
-        at = wt.at[kb, lax.rem(z + s, nz), r]
-        return copy(at, at, zd_send.at[s], zd_recv.at[s], z_device(-1))
+    middle = (rows // 2 + 15) // 16 * 16
+    parts = ((0, middle), (middle, rows - middle))
+
+    def up(s, slot, n):
+        at = wt.at[kb, lax.rem(z - s + nz, nz), r, pl.ds(*parts[n])]
+        return copy(at, at, zu_send.at[slot, n], zu_recv.at[slot, n], z_device(1))
+
+    def down(s, slot, n):
+        at = wt.at[kb, lax.rem(z + s, nz), r, pl.ds(*parts[n])]
+        return copy(at, at, zd_send.at[slot, n], zd_recv.at[slot, n], z_device(-1))
 
     def to_right(i):
         at = wt.at[kb, plane(i), r]
@@ -203,14 +199,15 @@
         to_left(i).start()
 
     def arrive(s):
-        up_in(s).wait_recv()
-        if s < half and s + 1 not in firsts:
-            up(s).start()
+        for n in range(2):
+            up(s, s, n).wait_recv()
+            if s < half:
+                up(s, s + 1, n).start()
+                down(s, s, n).wait_recv()
+                if s < half - 1:
+                    down(s, s + 1, n).start()
         spread(2 * s - 1)
         if s < half:
-            down_in(s).wait_recv()
-            if s < half - 1 and s + 1 not in firsts:
-                down(s).start()
             spread(2 * s)
 
     def hand_on(s):
@@ -276,24 +273,90 @@
             ctx[at, 0:TILE] = c0.astype(BF16)
             ctx[at, TILE:] = c1.astype(BF16)
 
-    def project(s):
+    def sides(part):
+        nothing = jnp.zeros((2 * rank, 2 * TILE), F32)
+        return jnp.concatenate([part, nothing, part], axis=0).T.astype(BF16)
+
+    def adapt():
+        both = tn(ab[...].reshape(hd, 2 * rank), ctx[...])
+        low[0:rank] = jnp.zeros((rank, 2 * TILE), BF16)
+        low[rank:] = both[0:rank].astype(BF16)
+        low_t[...] = sides(low[rank:].astype(F32))
+
+    def pack(g, w, wide):
+        for m in range(2):
+            lower = wide[m * rows + middle : (m + 1) * rows, 2 * rank :]
+            if 2 * middle > rows:
+                lower = jnp.concatenate([lower, jnp.zeros((2 * middle - rows, 2 * rank), F32)], axis=0)
+            grads[g, w, m] = (scale * (wide[m * rows : m * rows + middle, 0 : 2 * rank] + lower)).astype(BF16)
+
+    def trade(g, i):
+        w = plane(i)
+        return copy(grads.at[g, w, 1 - y_hi], theirs.at[g, w], yx_send.at[g, i], yx_recv.at[g, i], mate)
+
+    def give(g, i):
+        w = plane(i)
+        owner = (gossip, w * 2 + y_hi)
+        return copy(summed.at[g, w], landed.at[g, z], own_send.at[g, i], own_recv.at[g, z], owner)
+
+    def take(g, i):
+        w = plane(i)
+        owner = (gossip, w * 2 + y_hi)
+        return copy(summed.at[g, w], landed.at[g, w], own_send.at[g, i], own_recv.at[g, w], owner)
+
+    def pass_on(g, i):
+        w = plane(i)
+        trade(g, i).wait_recv()
+        summed[g, w] = (grads[g, w, y_hi].astype(F32) + theirs[g, w].astype(F32)).astype(BF16)
+        give(g, i).start()
+
+    def collect(g):
+        trade(g, 0).wait_recv()
+        total[g] = grads[g, z, y_hi].astype(F32) + theirs[g, z].astype(F32)
+
+        @pl.loop(1, nz)
+        def _(i):
+            take(g, i).wait_recv()
+            total[g] += landed[g, plane(i)].astype(F32)
+
+    based = []
+
+    def product(planes):
+        weights = [jnp.concatenate([wt[n, w].reshape(2 * rows, width) for w in planes], axis=0) for n in range(4)]
+        return nn(jnp.concatenate(weights, axis=1), ctx[...])
+
+    def prepare(s):
         members = [max(2 * s - 1, 0)] + ([2 * s] if 0 < s < half else [])
         for i in members:
             across_in(i).wait_recv()
         planes = [plane(i) for i in members]
+        out = product(planes)
+        for n, w in enumerate(planes):
+            base[w] = out[n * 2 * rows : (n + 1) * 2 * rows]
+        based.append(s)
+
+    def project(s):
+        members = [max(2 * s - 1, 0)] + ([2 * s] if 0 < s < half else [])
+        if s not in based:
+            for i in members:
+                across_in(i).wait_recv()
+        planes = [plane(i) for i in members]
 
         def rows_of(blocks):
             return jnp.concatenate([b.reshape(2 * rows, b.shape[-1]) for b in blocks], axis=0)
 
         factors = rows_of([ab[w] for w in planes])
         out = scale * nn(factors, low[...])
-        for n in range(4):
-            out += nn(rows_of([wt[n, w] for w in planes]), ctx[n * width : (n + 1) * width])
+        if s in based:
+            out += rows_of([base[w] for w in planes])
+        else:
+            out += product(planes)
         slope = jnp.tanh(SHARPNESS * out).astype(BF16)
         hid[...] += tn(factors, slope)
-        second = nn(slope, low_t[...])
+        wide = nn(slope, low_t[...])
         for n, w in enumerate(planes):
-            gb[w] = second[n * 2 * rows : (n + 1) * 2 * rows]
+            pack(0, w, wide[n * 2 * rows : (n + 1) * 2 * rows])
+            trade(0, members[n]).start()
 
     @pl.when(crosses)
     def _():
@@ -305,10 +368,10 @@
     def _():
         cross().wait_recv()
 
-    for s in reversed(firsts):
-        up(0, s).start()
-        if s < half:
-            down(0, s).start()
+    for n in range(2):
+        up(0, 1, n).start()
+        if half > 1:
+            down(0, 1, n).start()
     spread(0)
     for load in loads:
         load.wait()
@@ -323,91 +386,88 @@
     attend(cut[1], cut[2])
     chains = [range(a, b) for a, b in zip(firsts, (*firsts[1:], half + 1))]
     ticks = [[s for s in tick if s is not None] for tick in itertools.zip_longest(*chains)]
-    stages = [[0], *ticks]
-    for n, tick in enumerate(ticks):
-        for s in tick:
-            arrive(s)
-        for s in tick:
-            ab_in(s)
-        if n < 3:
-            attend(cut[n + 2], cut[n + 3])
-        for s in stages[n]:
-            hand_on(s)
-        for s in stages[n - 1] if n else ():
-            share(s)
-    for n in range(len(ticks), 3):
-        attend(cut[n + 2], cut[n + 3])
-
-    both = tn(ab[...].reshape(hd, 2 * rank), ctx[...])
-    low[0:rank] = jnp.zeros((rank, 2 * TILE), BF16)
-    low[rank:] = both[0:rank].astype(BF16)
-    low_t[...] = low[...].astype(F32).T.astype(BF16)
-
-    todo = [s for tick in stages[:-2] for s in tick]
-    later = stages[-2]
-    third = len(todo) // 3
-    for s in todo[:third]:
-        project(s)
-    for s in stages[-1]:
-        hand_on(s)
-    for s in later:
-        share(s)
-    for s in todo[third : 2 * third]:
-        project(s)
-    for s in stages[-1]:
-        share(s)
-    for s in [*todo[2 * third :], *later, *stages[-1]]:
-        project(s)
-
-    square[...] = jnp.zeros_like(square)
-    hid_t = jnp.concatenate([hid[rank:], jnp.zeros((rank, 2 * TILE), F32)], axis=0).T.astype(BF16)
-
-    def trade(i):
-        w = plane(i)
-        return copy(grads.at[w, 1 - y_hi], theirs.at[w], yx_send.at[i], yx_recv.at[i], mate)
-
-    def give(i):
-        w = plane(i)
-        return copy(summed.at[w], landed.at[z], own_send.at[i], own_recv.at[z], (gossip, w * 2 + y_hi))
-
-    def take(i):
-        w = plane(i)
-        return copy(summed.at[w], landed.at[w], own_send.at[i], own_recv.at[w], (gossip, w * 2 + y_hi))
+    todo, traded = [], []
+
+    def work_off(count):
+        for s in todo[:count]:
+            project(s)
+            traded.append([i for i in ((2 * s - 1, 2 * s) if s < half else (2 * s - 1,)) if i > 0])
+        del todo[:count]
+
+    def pass_off(count):
+        for group in traded[:count]:
+            for i in group:
+                pass_on(0, i)
+        del traded[:count]
+
+    for t in range(1, half + 1):
+        arrive(t)
+        if t <= len(ticks):
+            for s in ticks[t - 1]:
+                ab_in(s)
+        if t <= 3:
+            attend(cut[t + 1], cut[t + 2])
+        if t == len(ticks):
+            adapt()
+        hand_on(t - 1)
+        if t >= 2:
+            share(t - 2)
+            todo.append(t - 2)
+        if 3 <= t < half:
+            prepare(t - 3)
+        if t > len(ticks):
+            work_off(PLAN[t - len(ticks) - 1][0])
+            pass_off(PLAN[t - len(ticks) - 1][1])
+    for t in range(half, 3):
+        attend(cut[t + 2], cut[t + 3])
+    hand_on(half)
+    share(half - 1)
+    todo.append(half - 1)
+    pass_off(1)
+    work_off(len(todo) - 1)
+    pass_off(1)
+    share(half)
+    todo.append(half)
+    work_off(1)
+    pass_off(2)
+    work_off(len(todo))
+
+    hid_t = sides(hid[rank:])
 
     @pl.loop(0, nz)
     def _(n):
         i = nz - 1 - n
         w = plane(i)
         part = ctx[pl.ds(pl.multiple_of(w * 2 * rows, 2 * rows), 2 * rows)]
-        both = scale * (nn(part, hid_t) + gb[w])
-        grads[w] = both.astype(BF16).reshape(2, rows, 2 * rank)
-        trade(i).start()
+        pack(1, w, nn(part, hid_t))
+        trade(1, i).start()
+
+    pass_off(len(traded))
 
     @pl.loop(0, nz - 1)
     def _(n):
-        i = nz - 1 - n
-        w = plane(i)
-        trade(i).wait_recv()
-        summed[w] = (grads[w, y_hi].astype(F32) + theirs[w].astype(F32)).astype(BF16)
-        give(i).start()
-
-    trade(0).wait_recv()
-    moved[...] = grads[z, y_hi].astype(F32) + theirs[z].astype(F32)
-
-    @pl.loop(1, nz)
-    def _(i):
-        take(i).wait_recv()
-        moved[...] += landed[plane(i)].astype(F32)
-
-    moved[...] = abf[...] - STEP_RATE * moved[...]
+        pass_on(1, nz - 1 - n)
+
+    collect(0)
+    collect(1)
+
+    def unpack(g, turn):
+        straight, turned = total[g], pltpu.roll(total[g], rank, 1)
+        if turn:
+            straight, turned = turned, straight
+        return jnp.concatenate([straight, turned[0 : rows - middle]], axis=0)
+
+    column = lax.broadcasted_iota(jnp.int32, (rows, 2 * rank), 1)
+    gradient = jnp.where(column < rank, unpack(1, False), unpack(0, True))
+    moved[...] = abf[...] - STEP_RATE * gradient
     gossip_copy = copy(moved, partner, gos_sem.at[0], gos_sem.at[1], after)
     gossip_copy.start()
     gossip_copy.wait_recv()
     new = 0.5 * (moved[...] + partner[...])
+    square[...] = jnp.zeros_like(square)
     square[0:rows] = new
     turned = square[...].T
-    out_a[0] = turned[0:rank, 0:rows]
-    out_b[0] = turned[rank:, 0:rows]
+    out[...] = turned[:, 0:rows]
 
     gossip_copy.wait_send()
 
@@ -419,12 +479,14 @@
 
     @pl.loop(0, half)
     def _(s):
-        up(s).wait_send()
+        for n in range(2):
+            up(s, s + 1, n).wait_send()
         ab_up(s).wait_send()
 
     @pl.loop(0, half - 1)
     def _(s):
-        down(s).wait_send()
+        for n in range(2):
+            down(s, s + 1, n).wait_send()
         ab_down(s).wait_send()
 
     @pl.loop(0, nz)
@@ -433,11 +495,18 @@
         to_left(i).wait_send()
         on_in(i).wait_send()
         across(i).wait_send()
-        trade(i).wait_send()
+        trade(0, i).wait_send()
+        trade(1, i).wait_send()
 
     @pl.loop(1, nz)
     def _(i):
-        give(i).wait_send()
+        give(0, i).wait_send()
+        give(1, i).wait_send()
+
+
+def part_in_two(rank, both, upper, lower):
+    upper[0] = both[0:rank]
+    lower[0] = both[rank:]
 
 
 def solution(mesh):
@@ -449,40 +518,42 @@
         _, tokens, hd = queries.shape
         rows, rank = adapt_a.shape[1:]
         width = hd // 4
+        middle = (rows // 2 + 15) // 16 * 16
         dma = pltpu.SemaphoreType.DMA
         vmem = pltpu.VMEM
         whole = pl.BlockSpec(memory_space=pltpu.VMEM)
         place = pl.BlockSpec(memory_space=pl.ANY)
         flops = 2 * tokens * hd * (hd + 2 * tokens + 4 * rank)
-        new_a, new_b = pl.pallas_call(
+        new = pl.pallas_call(
             functools.partial(kernel, nz, n_gossip, hd, rank),
-            out_shape=(
-                jax.ShapeDtypeStruct((1, rank, rows), F32),
-                jax.ShapeDtypeStruct((1, rank, rows), F32),
-            ),
+            out_shape=jax.ShapeDtypeStruct((2 * rank, rows), F32),
             in_specs=[place, place, place, pl.BlockSpec(memory_space=pltpu.SMEM), place, whole, whole],
-            out_specs=(whole, whole),
+            out_specs=whole,
             scratch_shapes=[
                 vmem((tokens, hd), BF16), vmem((tokens, hd), BF16), vmem((tokens, hd), BF16),
                 vmem((4, nz, 2, rows, width), BF16),
                 vmem((nz, 2, rows, 2 * rank), BF16), vmem((rows, 2 * rank), F32), vmem((2 * rank, 128), F32),
                 vmem((TILE, 2 * TILE), F32), vmem((TILE, TILE), F32),
-                vmem((hd, tokens), BF16), vmem((2 * rank, tokens), BF16), vmem((tokens, 2 * rank), BF16),
-                vmem((2 * rank, tokens), F32), vmem((nz, 2 * rows, 2 * rank), F32),
-                vmem((nz, 2, rows, 2 * rank), BF16), vmem((nz, rows, 2 * rank), BF16),
-                vmem((nz, rows, 2 * rank), BF16), vmem((nz, rows, 2 * rank), BF16),
+                vmem((hd, tokens), BF16), vmem((2 * rank, tokens), BF16), vmem((tokens, 4 * rank), BF16),
+                vmem((nz, 2 * rows, tokens), F32), vmem((2 * rank, tokens), F32), vmem((2, nz, 2, middle, 2 * rank), BF16),
+                vmem((2, nz, middle, 2 * rank), BF16), vmem((2, nz, middle, 2 * rank), BF16),
+                vmem((2, nz, middle, 2 * rank), BF16), vmem((2, middle, 2 * rank), F32),
                 vmem((rows, 2 * rank), F32), vmem((rows, 2 * rank), F32),
                 dma((4,)), dma((2,)),
-                dma((half + 1,)), dma((half + 1,)), dma((half + 1,)), dma((half + 1,)),
+                dma((half + 1, 2)), dma((half + 1, 2)), dma((half + 1, 2)), dma((half + 1, 2)),
                 dma((nz,)), dma((nz,)), dma((nz,)), dma((nz,)), dma((nz,)), dma((nz,)), dma((nz,)), dma((nz,)),
                 dma((2,)), dma((half + 1,)), dma((half + 1,)), dma((half + 1,)), dma((half + 1,)),
-                dma((nz,)), dma((nz,)), dma((nz,)), dma((nz,)), dma((2,)),
+                dma((2, nz)), dma((2, nz)), dma((2, nz)), dma((2, nz)), dma((2,)),
             ],
             compiler_params=pltpu.CompilerParams(
                 collective_id=0, has_side_effects=True, vmem_limit_bytes=60 * 1024 * 1024
             ),
             cost_estimate=pl.CostEstimate(flops=flops, bytes_accessed=8 * tokens * hd, transcendentals=tokens * hd),
         )(queries, keys, values, pattern, out_weight.T, adapt_a.transpose(0, 2, 1), adapt_b)
+        half_shape = jax.ShapeDtypeStruct((1, rank, rows), F32)
+        new_a, new_b = pl.pallas_call(
+            functools.partial(part_in_two, rank), out_shape=(half_shape, half_shape), in_specs=[whole], out_specs=(whole, whole)
+        )(new)
         return new_a.transpose(0, 2, 1), new_b
 
     placed = (

time: 98.2 us -> 92.5 us (0.942)
  the two profiles are of different devices: /device:TPU:16 before, /device:TPU:1 now
where the time goes in v3:
time: 92.5 us; the launch traced here: 92.3 us
  Pallas kernels  91.7 us (99%)
    pallas_call x1, Pallas kernels, per_device(): pl.pallas_call(functools.partial(kernel, nz, n_gossip, hd, rank), out_sha...  90.2 us

profile of v3, /device:TPU:1, one launch (start us, length us, event | category | flops | bytes accessed | tf_op | source)
XLA Modules:
  0.0 92.3 jit_solution(10096860369889152915)
XLA Ops:
  0.6 90.2 %shard_map.86.both = f32[128,80]{1,0:T(8,128)} custom-call(bf16[1,256,2560]{2,1,0:T(8,128)(2,1)} %q_hbm.1, bf16[1,256,2560]{2,1,0:T(8,128)(2,1)} %k_hbm.1, bf16[1,256,2560]{2,1,0:T(8,128)(2,1)} %v_hbm.1, s32[1,2,3]{2,1,0:T(2,128)} %pattern.1, bf16[80,2560]{1,0:T(8,128)(2,1)} %bitcast.3, f32[1,64,80]{2,1,0:T(8,128)} %bitcast.4, f32[1,64,80]{2,1,0:T(8,128)} %b_ref.1), custom_call_target="tpu_custom_call" | custom-call | flops 4362076160 | bytes 5242880 | tf_op jit(solution)/shard_map/pallas_call | solution.py:527
  90.8 1.5 %shard_map.87 = (f32[1,64,80]{2,1,0:T(8,128)}, f32[1,64,80]{2,1,0:T(8,128)}) custom-call(f32[128,80]{1,0:T(8,128)} %shard_map.86.both), custom_call_target="tpu_custom_call" | custom-call | tf_op jit(solution)/shard_map/pallas_call | solution.py:554

commit v4 on v3

--- a/solution.py
+++ b/solution.py
@@ -35,9 +35,9 @@
 
 def kernel(
     nz, n_gossip, hd, rank,
-    q_hbm, k_hbm, v_hbm, pattern, w_hbm, a_ref, b_ref,
+    q_hbm, k_hbm, v_hbm, pattern_hbm, w_hbm, a_hbm, b_hbm,
     out,
-    q, k, v, wt, ab, abf, square, mask0, mask1, ctx, low, low_t, base, hid, grads, summed, theirs, landed, total, moved, partner,
+    q, k, v, pattern, factors_in, wt, ab, abf, square, mask0, mask1, ctx, low, low_t, base, hid, grads, summed, theirs, landed, total, moved, partner,
     load_sem, opp_sem, zu_send, zu_recv, zd_send, zd_recv,
     right_send, left_send, left_recv, right_recv, on_send, on_recv, sib_send, sib_recv,
     abp_sem, abu_send, abu_recv, abd_send, abd_recv,
@@ -117,12 +117,19 @@
     def _():
         own.start()
 
-    for load in loads:
+    small = [
+        pltpu.make_async_copy(a_hbm.at[0], factors_in.at[0], load_sem.at[4]),
+        pltpu.make_async_copy(b_hbm.at[0], factors_in.at[1], load_sem.at[5]),
+        pltpu.make_async_copy(pattern_hbm, pattern, load_sem.at[6]),
+    ]
+    for load in [*small, *loads]:
         load.start()
 
     square[...] = jnp.zeros_like(square)
-    square[0:rank, 0:rows] = a_ref[0]
-    square[rank:, 0:rows] = b_ref[0]
+    for load in small:
+        load.wait()
+    square[0:rank, 0:rows] = factors_in[0]
+    square[rank:, 0:rows] = factors_in[1]
     abf[...] = square[...].T[0:rows]
     ab[z, y_hi] = abf[...].astype(BF16)
 
@@ -200,12 +207,14 @@
 
     def arrive(s):
         for n in range(2):
-            up(s, s, n).wait_recv()
-            if s < half:
+            if s < half or n == 0:
+                up(s, s, n).wait_recv()
+            if s < half - 1 or (s < half and n == 0):
                 up(s, s + 1, n).start()
+            if s < half or n == 1:
                 down(s, s, n).wait_recv()
-                if s < half - 1:
-                    down(s, s + 1, n).start()
+            if s < half - 1 or (s < half and n == 1):
+                down(s, s + 1, n).start()
         spread(2 * s - 1)
         if s < half:
             spread(2 * s)
@@ -267,9 +276,10 @@
             e11 = jnp.exp2(s1 - top1)
             total0 = jnp.sum(e00, axis=0, keepdims=True)
             total1 = jnp.sum(e01, axis=0, keepdims=True) + jnp.sum(e11, axis=0, keepdims=True)
+            part0, part1 = 1.0 / total0, 1.0 / total1
             v0, v1 = v[0:TILE, at], v[TILE:, at]
-            c0 = tn(v0, e00.astype(BF16)) / total0
-            c1 = (tn(v0, e01.astype(BF16)) + tn(v1, e11.astype(BF16))) / total1
+            c0 = tn(v0, (e00 * part0).astype(BF16))
+            c1 = tn(v0, (e01 * part1).astype(BF16)) + tn(v1, (e11 * part1).astype(BF16))
             ctx[at, 0:TILE] = c0.astype(BF16)
             ctx[at, TILE:] = c1.astype(BF16)
 
@@ -370,8 +380,7 @@
 
     for n in range(2):
         up(0, 1, n).start()
-        if half > 1:
-            down(0, 1, n).start()
+        down(0, 1, n).start()
     spread(0)
     for load in loads:
         load.wait()
@@ -434,15 +443,16 @@
 
     hid_t = sides(hid[rank:])
 
-    @pl.loop(0, nz)
-    def _(n):
+    def send_a(n):
         i = nz - 1 - n
         w = plane(i)
         part = ctx[pl.ds(pl.multiple_of(w * 2 * rows, 2 * rows), 2 * rows)]
         pack(1, w, nn(part, hid_t))
         trade(1, i).start()
 
+    pl.loop(0, half)(send_a)
     pass_off(len(traded))
+    pl.loop(half, nz)(send_a)
 
     @pl.loop(0, nz - 1)
     def _(n):
@@ -477,15 +487,17 @@
 
     ab_mate(y_hi).wait_send()
 
+    up(half - 1, half, 0).wait_send()
+    down(half - 1, half, 1).wait_send()
+
     @pl.loop(0, half)
+    def _(s):
+        ab_up(s).wait_send()
+
+    @pl.loop(0, half - 1)
     def _(s):
         for n in range(2):
             up(s, s + 1, n).wait_send()
-        ab_up(s).wait_send()
-
-    @pl.loop(0, half - 1)
-    def _(s):
-        for n in range(2):
             down(s, s + 1, n).wait_send()
         ab_down(s).wait_send()
 
@@ -527,10 +539,11 @@
         new = pl.pallas_call(
             functools.partial(kernel, nz, n_gossip, hd, rank),
             out_shape=jax.ShapeDtypeStruct((2 * rank, rows), F32),
-            in_specs=[place, place, place, pl.BlockSpec(memory_space=pltpu.SMEM), place, whole, whole],
+            in_specs=[place] * 7,
             out_specs=whole,
             scratch_shapes=[
                 vmem((tokens, hd), BF16), vmem((tokens, hd), BF16), vmem((tokens, hd), BF16),
+                pltpu.SMEM(pattern.shape, jnp.int32), vmem((2, rank, rows), F32),
                 vmem((4, nz, 2, rows, width), BF16),
                 vmem((nz, 2, rows, 2 * rank), BF16), vmem((rows, 2 * rank), F32), vmem((2 * rank, 128), F32),
                 vmem((TILE, 2 * TILE), F32), vmem((TILE, TILE), F32),
@@ -539,7 +552,7 @@
                 vmem((2, nz, middle, 2 * rank), BF16), vmem((2, nz, middle, 2 * rank), BF16),
                 vmem((2, nz, middle, 2 * rank), BF16), vmem((2, middle, 2 * rank), F32),
                 vmem((rows, 2 * rank), F32), vmem((rows, 2 * rank), F32),
-                dma((4,)), dma((2,)),
+                dma((7,)), dma((2,)),
                 dma((half + 1, 2)), dma((half + 1, 2)), dma((half + 1, 2)), dma((half + 1, 2)),
                 dma((nz,)), dma((nz,)), dma((nz,)), dma((nz,)), dma((nz,)), dma((nz,)), dma((nz,)), dma((nz,)),
                 dma((2,)), dma((half + 1,)), dma((half + 1,)), dma((half + 1,)), dma((half + 1,)),

time: 92.5 us -> 90.9 us (0.983)
  Pallas kernels: 91.7 us -> 89.4 us
    pallas_call x1, Pallas kernels: 90.2 us -> 87.9 us  [per_device(): pl.pallas_call(functools.partial(kernel, nz, n_gossip, hd, rank), out_sha...]
where the time goes in v4:
time: 90.9 us; the launch traced here: 90 us
  Pallas kernels  89.4 us (98%)
    pallas_call x1, Pallas kernels, per_device(): pl.pallas_call(functools.partial(kernel, nz, n_gossip, hd, rank), out_sha...  87.9 us

profile of v4, /device:TPU:1, one launch (start us, length us, event | category | flops | bytes accessed | tf_op | source)
XLA Modules:
  0.0 90.0 jit_solution(18012234255158985941)
XLA Ops:
  0.6 87.9 %shard_map.86.both = f32[128,80]{1,0:T(8,128)} custom-call(bf16[1,256,2560]{2,1,0:T(8,128)(2,1)} %q_hbm.1, bf16[1,256,2560]{2,1,0:T(8,128)(2,1)} %k_hbm.1, bf16[1,256,2560]{2,1,0:T(8,128)(2,1)} %v_hbm.1, s32[1,2,3]{2,1,0:T(2,128)} %pattern_hbm.1, bf16[80,2560]{1,0:T(8,128)(2,1)} %bitcast.3, f32[1,64,80]{2,1,0:T(8,128)} %bitcast.4, f32[1,64,80]{2,1,0:T(8,128)} %b_hbm.1), custom_call_target="tpu_custom_call" | custom-call | flops 4362076160 | bytes 5242880 | tf_op jit(solution)/shard_map/pallas_call | solution.py:539
  88.6 1.5 %shard_map.87 = (f32[1,64,80]{2,1,0:T(8,128)}, f32[1,64,80]{2,1,0:T(8,128)}) custom-call(f32[128,80]{1,0:T(8,128)} %shard_map.86.both), custom_call_target="tpu_custom_call" | custom-call | tf_op jit(solution)/shard_map/pallas_call | solution.py:567

commit v5 on v4

--- a/solution.py
+++ b/solution.py
@@ -472,14 +472,6 @@
     moved[...] = abf[...] - STEP_RATE * gradient
     gossip_copy = copy(moved, partner, gos_sem.at[0], gos_sem.at[1], after)
     gossip_copy.start()
-    gossip_copy.wait_recv()
-    new = 0.5 * (moved[...] + partner[...])
-    square[...] = jnp.zeros_like(square)
-    square[0:rows] = new
-    turned = square[...].T
-    out[...] = turned[:, 0:rows]
-
-    gossip_copy.wait_send()
 
     @pl.when(crosses)
     def _():
@@ -514,6 +506,14 @@
     def _(i):
         give(0, i).wait_send()
         give(1, i).wait_send()
+
+    gossip_copy.wait_recv()
+    new = 0.5 * (moved[...] + partner[...])
+    square[...] = jnp.zeros_like(square)
+    square[0:rows] = new
+    turned = square[...].T
+    out[...] = turned[:, 0:rows]
+    gossip_copy.wait_send()
 
 
 def part_in_two(rank, both, upper, lower):

time: 90.9 us -> 90.4 us (level)
  no operation moved by 1% of the time
where the time goes in v5:
time: 90.4 us; the launch traced here: 89.6 us
  Pallas kernels  89 us (98%)
    pallas_call x1, Pallas kernels, per_device(): pl.pallas_call(functools.partial(kernel, nz, n_gossip, hd, rank), out_sha...  87.5 us

profile of v5, /device:TPU:1, one launch (start us, length us, event | category | flops | bytes accessed | tf_op | source)
XLA Modules:
  0.0 89.6 jit_solution(12614135050402173267)
XLA Ops:
  0.6 87.5 %shard_map.86.both = f32[128,80]{1,0:T(8,128)} custom-call(bf16[1,256,2560]{2,1,0:T(8,128)(2,1)} %q_hbm.1, bf16[1,256,2560]{2,1,0:T(8,128)(2,1)} %k_hbm.1, bf16[1,256,2560]{2,1,0:T(8,128)(2,1)} %v_hbm.1, s32[1,2,3]{2,1,0:T(2,128)} %pattern_hbm.1, bf16[80,2560]{1,0:T(8,128)(2,1)} %bitcast.3, f32[1,64,80]{2,1,0:T(8,128)} %bitcast.4, f32[1,64,80]{2,1,0:T(8,128)} %b_hbm.1), custom_call_target="tpu_custom_call" | custom-call | flops 4362076160 | bytes 5242880 | tf_op jit(solution)/shard_map/pallas_call | solution.py:539
  88.1 1.5 %shard_map.87 = (f32[1,64,80]{2,1,0:T(8,128)}, f32[1,64,80]{2,1,0:T(8,128)}) custom-call(f32[128,80]{1,0:T(8,128)} %shard_map.86.both), custom_call_target="tpu_custom_call" | custom-call | tf_op jit(solution)/shard_map/pallas_call | solution.py:567
